TPU v7x, 1024 devices: a whole 4x4x32 slice. The times are simulated.
1024 devices in a mesh: dp: 2 (over core), expert: 64 (over x_lo, z), tensor: 8 (over y, x_hi).
Axes of the slice: x: 4 (x_hi: 2, x_lo: 2; x = x_hi * 2 + x_lo), y: 4, z: 32, core: 2. Of those that a mesh axis runs over, the one named last changes fastest.
Arguments:
- residual: bfloat16 [16384, 4096], P(('dp', 'expert'), 'tensor'), may hold values from -6 to 6
- route_ids: int32 [16384, 2], P(('dp', 'expert')), may hold values from 0 to 63, all different within a row
- slot_hidden: bfloat16 [32768, 2560], P(('dp', 'expert')), may hold values from -6 to 6
- slot_gates: float32 [32768], P(('dp', 'expert')), may hold values from 0.1 to 1
- down_weight: bfloat16 [64, 2560, 4096], P('expert', None, 'tensor'), may hold values from -0.125 to 0.125
- cotangent: bfloat16 [16384, 4096], P(('dp', 'expert'), 'tensor'), may hold values from -3 to 3
Outputs:
- combined: bfloat16 [16384, 4096], P(('dp', 'expert'), 'tensor')
- hidden_grad: bfloat16 [32768, 2560], P(('dp', 'expert'), 'tensor')
- gate_grad: float32 [32768], P(('dp', 'expert', 'tensor'))
- down_weight_gradient: bfloat16 [64, 2560, 4096], P('expert', 'dp', 'tensor')
Inputs may be any that keep to these rules, and one draw needn't show every extreme that they name: `route_ids`: the two experts of a token differ.
All inputs are finite; a program needn't handle non-finite values.
Results may differ from a plain program's by a relative error of at most 0.022.
Values may be sent and summed in bfloat16 or wider, within the bound.
No kernel may reach another device: no remote copies, remote signals or barrier semaphores. Data moves between devices by JAX's collectives and lax.ppermute only.
A program may use at most 64 MiB of HBM per device.

v0:
```python
import jax
import jax.numpy as jnp
from jax import lax
from jax.sharding import PartitionSpec as P


def on_device(residual, route_ids, slot_hidden, slot_gates, down_weight, cotangent):
    tok_rows = residual.shape[0]
    experts = lax.axis_size("expert")
    expert_capacity = slot_hidden.shape[0]
    per_source = expert_capacity // experts
    weight = down_weight[0]
    flat_ids = route_ids.reshape(-1)
    expert_iota = jnp.arange(experts, dtype=jnp.int32)
    onehot = (flat_ids[:, None] == expert_iota[None, :]).astype(jnp.int32)
    before = jnp.cumsum(onehot, axis=0) - onehot
    rank_of = jnp.sum(before * onehot, axis=1)
    kept_mask = rank_of < per_source
    target = flat_ids * per_source + rank_of
    slot_iota = jnp.arange(expert_capacity, dtype=jnp.int32)
    hit_table = jnp.logical_and(kept_mask[:, None], target[:, None] == slot_iota[None, :])
    placing = jnp.sum(
        hit_table.reshape(tok_rows, 2, expert_capacity).astype(jnp.int32), axis=1
    ).astype(jnp.bfloat16)
    gate_column = slot_gates[:, None]
    projected = jnp.dot(slot_hidden, weight, preferred_element_type=jnp.float32)
    outgoing = (gate_column * projected).astype(jnp.bfloat16)
    arrived = lax.all_to_all(outgoing, "expert", split_axis=0, concat_axis=0, tiled=True)
    combined = (
        residual.astype(jnp.float32) + jnp.dot(placing, arrived, preferred_element_type=jnp.float32)
    ).astype(jnp.bfloat16)
    sending = lax.dot_general(
        placing, cotangent, (((0,), (0,)), ((), ())), preferred_element_type=jnp.float32
    ).astype(jnp.bfloat16)
    slot_grad = lax.all_to_all(sending, "expert", split_axis=0, concat_axis=0, tiled=True)
    scaled = (gate_column * slot_grad.astype(jnp.float32)).astype(jnp.bfloat16)
    hidden_terms = lax.dot_general(
        scaled, weight, (((1,), (1,)), ((), ())), preferred_element_type=jnp.float32
    )
    gate_terms = jnp.sum(slot_grad.astype(jnp.float32) * projected, axis=1)
    hidden_grad, gate_grad = (
        lax.psum_scatter(
            hidden_terms.astype(jnp.bfloat16), "tensor", scatter_dimension=1, tiled=True
        ).astype(jnp.float32),
        lax.psum_scatter(
            gate_terms.astype(jnp.bfloat16), "tensor", scatter_dimension=0, tiled=True
        ).astype(jnp.float32),
    )
    partial_value = lax.dot_general(
        slot_hidden, scaled, (((0,), (0,)), ((), ())), preferred_element_type=jnp.float32
    )
    down_weight_gradient = lax.psum_scatter(
        partial_value.astype(jnp.bfloat16), "dp", scatter_dimension=0, tiled=True
    )
    return (combined, hidden_grad.astype(jnp.bfloat16), gate_grad, down_weight_gradient[None])


def solution(mesh):
    placed = (
        P(("dp", "expert"), "tensor"),
        P(("dp", "expert"), None),
        P(("dp", "expert"), None),
        P(("dp", "expert")),
        P("expert", None, "tensor"),
        P(("dp", "expert"), "tensor"),
    )
    return jax.shard_map(
        on_device,
        mesh=mesh,
        in_specs=placed,
        out_specs=(
            P(("dp", "expert"), "tensor"),
            P(("dp", "expert"), "tensor"),
            P(("dp", "expert", "tensor")),
            P("expert", "dp", "tensor"),
        ),
        check_vma=False,
    )
```

profile of v0, /device:TPU:1, one launch (start us, length us, event | category | flops | bytes accessed | tf_op | source)
XLA Modules:
  0.0 224.6 jit_solution(6552507581442356630)
XLA Ops:
  7.2 0.0 copy-start
  7.2 0.0 copy-start.1
  7.2 0.0 reduce-scatter.5.cloned.1.call-start
  7.2 0.9 copy.33
  8.2 0.1 eq.43
  8.3 0.1 eq.39
  8.5 0.6 reduce-window.6
  9.1 0.2 slice_reduce_fusion
  9.3 0.1 fusion.9
  9.4 0.1 reduce_sum.30
  9.6 0.1 copy.36
  9.6 0.7 multiply_add_fusion
  10.3 0.1 convert_reduce_fusion
  10.5 1.2 convolution_convert_fusion.2
  11.6 0.1 all_to_all.17
  11.7 67.8 %all_to_all.21 = bf16[64,4,512]{2,1,0:T(4,128)(2,1)S(1)} all-to-all(bf16[64,4,512]{2,1,0:T(4,128)(2,1)S(1)} %all_to_all.17), channel_id=1, replica_groups=mesh['dp'=2,'expert'=64,'tensor'=8] {'expert'}, dimensions={0} | all-to-all | bytes 524288 | tf_op jit(solution)/shard_map/all_to_all | solution.py:35
  79.5 0.0 copy-done.1
  79.5 3.8 %fusion = bf16[2560,512]{0,1:T(8,128)(2,1)} fusion(bf16[256,2560]{1,0:T(8,128)(2,1)} %param.8, f32[256,512]{1,0:T(8,128)S(1)} %reshape.65, f32[256]{0:T(256)S(1)} %copy-done.1), kind=kOutput, calls=%fused_computation.1 | convolution fusion | flops 672661504 | bytes 4457472 | tf_op jit(solution)/shard_map/dot_general | solution.py:49
  83.3 0.0 reduce-scatter.5.cloned.1.call-update
  83.3 0.0 reduce-scatter.3.cloned.1.call-start
  83.4 0.7 mul.38
  84.1 1.6 multiply_convert_fusion.1
  85.7 1.0 convert_element_type.70
  86.8 0.0 copy-done
  86.8 2.0 convolution_convert_fusion.1
  88.7 0.0 reduce-scatter.3.cloned.1.call-update
  88.8 2.3 %multiply_reduce_fusion = (bf16[256]{0:T(256)(128)(2,1)S(1)}, bf16[256,512]{1,0:T(8,128)(2,1)S(1)}) fusion(f32[256,512]{1,0:T(8,128)S(1)} %reshape.65, f32[256]{0:T(256)S(1)} %copy-done.1, bf16[256,2560]{1,0:T(8,128)(2,1)} %param.8, bf16[1,2560,512]{2,1,0:T(8,128)(2,1)S(1)} %copy-done), kind=kOutput, calls=%fused_computation.10 | convolution fusion | flops 671612672 | bytes 4720128 | tf_op jit(solution)/shard_map/dot_general | solution.py:26
  91.0 0.8 all_to_all.14
  91.8 8.8 %all-to-all-start = ((bf16[64,4,512]{2,1,0:T(4,128)(2,1)}), bf16[64,4,512]{2,1,0:T(4,128)(2,1)S(1)}, u32[]{:S(2)}, u32[]{:S(2)}) async-start(bf16[64,4,512]{2,1,0:T(4,128)(2,1)} %all_to_all.14), calls=%async_computation | async-start | bytes 524288 | tf_op jit(solution)/shard_map/all_to_all | solution.py:28
  100.6 1.3 dynamic-slice
  102.5 21.7 %all-reduce = bf16[256]{0:T(256)(128)(2,1)S(1)} all-reduce(bf16[256]{0:T(256)(128)(2,1)S(1)} %get-tuple-element.24), channel_id=3, replica_groups=mesh['dp'=2,'expert'=64,'tensor'=8] {'tensor'}, use_global_device_ids=true, to_apply=%region_6.7.clone | all-reduce | flops 256 | bytes 1024
  124.2 0.6 dynamic-slice_convert_fusion
  124.8 12.6 %all-to-all-done = bf16[64,4,512]{2,1,0:T(4,128)(2,1)S(1)} async-done(((bf16[64,4,512]{2,1,0:T(4,128)(2,1)}), bf16[64,4,512]{2,1,0:T(4,128)(2,1)S(1)}, u32[]{:S(2)}, u32[]{:S(2)}) %all-to-all-start) | async-done | bytes 262176 | tf_op jit(solution)/shard_map/all_to_all | solution.py:28
  137.4 0.1 all_to_all.16
  137.4 1.8 fusion.4
  139.2 0.0 reduce-scatter.5.cloned.1.call-done
  139.2 2.4 %copy.38 = bf16[1,1280,512]{2,1,0:T(8,128)(2,1)} copy(bf16[1,1280,512]{1,2,0:T(8,128)(2,1)} %bitcast.35) | data formatting | bytes 2621440
  141.6 76.2 %reduce-scatter.3.cloned.1.call-done = bf16[256,320]{0,1:T(8,128)(2,1)} async-done(((bf16[256,2560]{0,1:T(8,128)(2,1)}), bf16[256,320]{0,1:T(8,128)(2,1)}) %reduce-scatter.3.cloned.1.call-update) | async-done | bytes 163856 | tf_op jit(solution)/shard_map/reduce_scatter | solution.py:42
  (5 shorter events, 0.1 us)
Async XLA Ops:
  7.2 79.6 %copy-start = (bf16[1,2560,512]{2,1,0:T(8,128)(2,1)S(1)}, bf16[1,2560,512]{2,1,0:T(8,128)(2,1)}, u32[]{:S(2)}) copy-start(bf16[1,2560,512]{2,1,0:T(8,128)(2,1)} %param.10) | copy-start | bytes 7864324
  7.2 72.3 %copy-start.1 = (f32[256]{0:T(256)S(1)}, f32[256]{0:T(256)}, u32[]{:S(2)}) copy-start(f32[256]{0:T(256)} %param.9) | copy-start | bytes 3076
  7.2 132.0 %reduce-scatter.5.cloned.1.call-start = ((), (), s32[]{:S(2)}) async-start(), calls=%async_computation.5 | async-start | bytes 3932160 | tf_op jit(solution)/shard_map/reduce_scatter | solution.py:52
  83.3 134.4 %reduce-scatter.3.cloned.1.call-start = ((), (), s32[]{:S(2)}) async-start(), calls=%async_computation.4 | async-start | bytes 1474560 | tf_op jit(solution)/shard_map/reduce_scatter | solution.py:42
  91.8 45.6 %all-to-all-start = ((bf16[64,4,512]{2,1,0:T(4,128)(2,1)}), bf16[64,4,512]{2,1,0:T(4,128)(2,1)S(1)}, u32[]{:S(2)}, u32[]{:S(2)}) async-start(bf16[64,4,512]{2,1,0:T(4,128)(2,1)} %all_to_all.14), calls=%async_computation | async-start | bytes 524288 | tf_op jit(solution)/shard_map/all_to_all | solution.py:28
Sparse Core Ops, SparseCore 0:
  83.5 20.7 reduce-scatter.4
  111.5 106.2 reduce-scatter.2
where the time goes:
time: 225 us
  blocking collectives  89.4 us (40%)
  waiting for transfers between devices  88.8 us (39%)
  between operations  14.8 us (7%)
  matrix products  10.9 us (5%)
  starting transfers between devices  8.87 us (4%)
  local copies, waits for them, and re-layouts  8 us (4%)
  other arithmetic  3.84 us (2%)
    reduce_scatter x1, waiting for transfers between devices, on_device(): lax.psum_scatter(hidden_terms.astype(jnp.bfloat16), 'tensor', scatter_dim...  76.2 us
    all_to_all x1, blocking collectives, on_device(): lax.all_to_all(sending, 'expert', split_axis=0, concat_axis=0, tiled=True)  67.8 us
    unnamed x1, blocking collectives  21.7 us
    all_to_all x1, waiting for transfers between devices, on_device(): lax.all_to_all(outgoing, 'expert', split_axis=0, concat_axis=0, tiled=True)  12.6 us
    all_to_all x1, starting transfers between devices, on_device(): lax.all_to_all(outgoing, 'expert', split_axis=0, concat_axis=0, tiled=True)  8.79 us
    unnamed x7, local copies, waits for them, and re-layouts  4.65 us
  transfers between devices with their start and end apart: 3, of which 2 were waited for; matrix products, arithmetic and copies ran while one was open for 6% of the time, Pallas kernels for 0%

commit v1 on v0

v1 whole, which is shorter than its diff:
```python
import jax
import jax.numpy as jnp
from jax import lax
from jax.experimental import pallas as pl
from jax.experimental.pallas import tpu as pltpu
from jax.sharding import PartitionSpec as P

F32 = jnp.float32
BF16 = jnp.bfloat16
EXTRA = 16


def iota(shape, dim):
    return lax.broadcasted_iota(jnp.int32, shape, dim)


def column_of(row):
    n = row.shape[1]
    same = iota((n, n), 0) == iota((n, n), 1)
    return jnp.sum(jnp.where(same, jnp.broadcast_to(row, (n, n)), 0.0), axis=1, keepdims=True)


def route_hits(ids, experts, per):
    tokens = ids.shape[1]
    rows = experts * 2 * per
    slot = iota((rows, tokens), 0)
    owner = slot // (2 * per)
    place = slot % (2 * per)
    named = jnp.logical_or(ids[0:1, :] == owner, ids[1:2, :] == owner)
    earlier = (iota((tokens, tokens), 0) < iota((tokens, tokens), 1)).astype(F32).astype(BF16)
    rank = jnp.dot(named.astype(F32).astype(BF16), earlier, preferred_element_type=F32).astype(jnp.int32)
    send = jnp.logical_and(named, rank == place)
    send = jnp.logical_and(send, place < per)
    take = jnp.logical_and(named, rank + per == place)
    return send.astype(F32).astype(BF16), take.astype(F32).astype(BF16)


def spread(slots, per, offset):
    row, slot = iota((2 * slots, slots), 0), iota((2 * slots, slots), 1)
    return ((slot // per) * 2 * per + offset + slot % per == row).astype(F32).astype(BF16)


def send_kernel(experts, per, ids, cotangent, hidden, weight, gates, message, take, projected):
    gate = column_of(gates[...])
    product = jnp.dot(hidden[...], weight[...], preferred_element_type=F32)
    projected[...] = product
    outgoing = (gate * product).astype(BF16)
    send_hits, take_hits = route_hits(ids[...], experts, per)
    take[...] = take_hits
    slots = experts * per
    rows = jnp.dot(send_hits, cotangent[...], preferred_element_type=F32)
    rows += jnp.dot(spread(slots, per, per), outgoing, preferred_element_type=F32)
    message[...] = rows.astype(BF16)


def hidden_kernel(experts, per, parts, arrived, weight, gates, projected, scaled, partial):
    slots = experts * per
    gate = column_of(gates[...])
    slot_grad = lax.dot_general(
        spread(slots, per, 0), arrived[...], (((0,), (0,)), ((), ())), preferred_element_type=F32
    )
    grown = (gate * slot_grad).astype(BF16)
    scaled[...] = grown
    terms = jnp.sum(slot_grad * projected[...], axis=1, keepdims=True).astype(BF16).astype(F32)
    width = slots // parts
    chosen = (iota((parts, slots), 1) // width == iota((parts, slots), 0)).astype(F32).astype(BF16)
    lanes = jnp.where(iota((slots, slots), 0) % width == iota((slots, slots), 1), terms, 0.0).astype(BF16)
    gate_rows = jnp.dot(chosen, lanes, preferred_element_type=F32)
    block = weight.shape[0] // parts
    for part in range(parts):
        partial[part, :block, :] = lax.dot_general(
            weight[part * block : (part + 1) * block, :], grown, (((1,), (1,)), ((), ())),
            preferred_element_type=F32,
        ).astype(BF16)
        tail = jnp.where(iota((EXTRA, slots), 0) == 0, gate_rows[part : part + 1, :], 0.0)
        partial[part, block:, :] = tail.astype(BF16)


def weight_kernel(hidden, scaled, out):
    step = 512
    for begin in range(0, hidden.shape[1], step):
        out[begin : begin + step, :] = lax.dot_general(
            hidden[:, begin : begin + step], scaled[...], (((0,), (0,)), ((), ())), preferred_element_type=F32
        ).astype(BF16)


def combine_kernel(arrived, take, residual, out):
    reduced = lax.dot_general(take[...], arrived[...], (((0,), (0,)), ((), ())), preferred_element_type=F32)
    out[...] = (residual[...].astype(F32) + reduced).astype(BF16)


def sum_kernel(parts, partial, hidden_grad, gate_grad):
    block, width = hidden_grad.shape[0], gate_grad.shape[1]
    total = partial[0, :block, :].astype(F32)
    gate = partial[0, block:, :].astype(F32)
    for part in range(1, parts):
        total += partial[part, :block, :].astype(F32)
        gate += partial[part, block:, :].astype(F32)
    hidden_grad[...] = total.astype(BF16)
    gate_grad[...] = gate[0:1, :width]


def call(kernel, outs, *args):
    return pl.pallas_call(
        kernel,
        out_shape=[jax.ShapeDtypeStruct(shape, dtype) for shape, dtype in outs],
        in_specs=[pl.BlockSpec(memory_space=pltpu.VMEM)] * len(args),
        out_specs=[pl.BlockSpec(memory_space=pltpu.VMEM)] * len(outs),
        compiler_params=pltpu.CompilerParams(vmem_limit_bytes=40 * 1024 * 1024),
    )(*args)


def on_device(residual, route_ids, slot_hidden, slot_gates, down_weight, cotangent):
    tokens, width = residual.shape
    experts, parts = lax.axis_size("expert"), lax.axis_size("tensor")
    slots, inner = slot_hidden.shape
    per = slots // experts
    weight = down_weight[0]
    gates = slot_gates[None, :]

    def bind(kernel, *sizes):
        return lambda *refs: kernel(*sizes, *refs)

    message, take, projected = call(
        bind(send_kernel, experts, per),
        [((2 * slots, width), BF16), ((2 * slots, tokens), BF16), ((slots, width), F32)],
        route_ids.T, cotangent, slot_hidden, weight, gates,
    )
    arrived = lax.all_to_all(
        message.reshape(experts, 2 * per, width), "expert", split_axis=0, concat_axis=0, tiled=True
    ).reshape(2 * slots, width)
    scaled, partial = call(
        bind(hidden_kernel, experts, per, parts),
        [((slots, width), BF16), ((parts, inner // parts + EXTRA, slots), BF16)],
        arrived, weight, gates, projected,
    )
    partial = lax.all_to_all(partial, "tensor", split_axis=0, concat_axis=0, tiled=True)
    (weight_terms,) = call(weight_kernel, [((inner, width), BF16)], slot_hidden, scaled)
    weight_grad = lax.psum_scatter(weight_terms, "dp", scatter_dimension=0, tiled=True)
    (combined,) = call(combine_kernel, [((tokens, width), BF16)], arrived, take, residual)
    hidden_grad, gate_grad = call(
        bind(sum_kernel, parts), [((inner // parts, slots), BF16), ((1, slots // parts), F32)], partial
    )
    return combined, hidden_grad.T, gate_grad[0], weight_grad[None]


def solution(mesh):
    placed = (
        P(("dp", "expert"), "tensor"),
        P(("dp", "expert"), None),
        P(("dp", "expert"), None),
        P(("dp", "expert")),
        P("expert", None, "tensor"),
        P(("dp", "expert"), "tensor"),
    )
    return jax.shard_map(
        on_device,
        mesh=mesh,
        in_specs=placed,
        out_specs=(
            P(("dp", "expert"), "tensor"),
            P(("dp", "expert"), "tensor"),
            P(("dp", "expert", "tensor")),
            P("expert", "dp", "tensor"),
        ),
        check_vma=False,
    )
```

time: 225 us -> 144 us (0.64)
  the two profiles are of different devices: /device:TPU:1 before, /device:TPU:96 now
where the time goes in v1:
time: 144 us
  blocking collectives  90.7 us (63%)
  waiting for transfers between devices  19.1 us (13%)
  between operations  14.1 us (10%)
  Pallas kernels  7.88 us (5%)
  starting transfers between devices  6.81 us (5%)
  local copies, waits for them, and re-layouts  5.33 us (4%)
    all_to_all x1, blocking collectives, on_device(): lax.all_to_all(message.reshape(experts, 2 * per, width), 'expert', split_...  90.7 us
    all_to_all x1, waiting for transfers between devices, on_device(): lax.all_to_all(partial, 'tensor', split_axis=0, concat_axis=0, tiled=True)  19.1 us
    pallas_call x5, Pallas kernels, call(): pl.pallas_call(kernel, out_shape=[jax.ShapeDtypeStruct(shape, dtype) for...  7.88 us
    all_to_all x1, starting transfers between devices, on_device(): lax.all_to_all(partial, 'tensor', split_axis=0, concat_axis=0, tiled=True)  6.77 us
    unnamed x18, local copies, waits for them, and re-layouts  5.33 us
  transfers between devices with their start and end apart: 2, of which 1 were waited for; matrix products, arithmetic and copies ran while one was open for 0% of the time, Pallas kernels for 1%

profile of v1, /device:TPU:96, one launch (start us, length us, event | category | flops | bytes accessed | tf_op | source)
XLA Modules:
  0.0 143.8 jit_solution(2943000200872073029)
XLA Ops:
  7.2 0.0 reduce-scatter.2.cloned.1.call-start
  7.2 0.0 copy-start
  7.2 1.7 %copy-done = bf16[1,2560,512]{2,1,0:T(8,128)(2,1)S(1)} copy-done((bf16[1,2560,512]{2,1,0:T(8,128)(2,1)S(1)}, bf16[1,2560,512]{2,1,0:T(8,128)(2,1)}, u32[]{:S(2)}) %copy-start) | copy-done | bytes 2621464
  9.0 0.0 copy-start.2
  9.0 1.3 copy-done.2
  10.3 0.0 copy-start.4
  10.3 0.9 copy-done.4
  11.2 0.0 copy-start.6
  11.2 0.7 copy-done.6
  11.9 0.0 copy-start.8
  11.9 0.7 copy-done.8
  12.5 0.0 copy-start.1
  12.5 0.0 copy-start.7
  12.5 1.3 shard_map.93
  13.9 90.7 %all_to_all.10 = bf16[64,8,512]{2,1,0:T(8,128)(2,1)S(1)} all-to-all(bf16[64,8,512]{2,1,0:T(8,128)(2,1)S(1)} %bitcast.12), channel_id=1, replica_groups=mesh['dp'=2,'expert'=64,'tensor'=8] {'expert'}, dimensions={0} | all-to-all | bytes 1048576 | tf_op jit(solution)/shard_map/all_to_all | solution.py:129
  104.5 0.0 copy-done.1
  104.5 0.0 copy-done.7
  104.5 0.0 copy-start.3
  104.5 2.4 %shard_map.95 = (bf16[256,512]{1,0:T(8,128)(2,1)S(1)}, bf16[8,336,256]{2,1,0:T(8,128)(2,1)}) custom-call(bf16[512,512]{1,0:T(8,128)(2,1)S(1)} %bitcast.10, bf16[2560,512]{1,0:T(8,128)(2,1)S(1)} %bitcast.9, f32[1,256]{1,0:T(1,128)S(1)} %bitcast.14, f32[256,512]{1,0:T(8,128)S(1)} %get-tuple-element.13.refs_3_), custom_call_target="tpu_custom_call" | custom-call | tf_op jit(solution)/shard_map/pallas_call | solution.py:104
  107.0 0.0 copy-done.3
  107.0 2.4 %shard_map.97 = bf16[2560,512]{1,0:T(8,128)(2,1)} custom-call(bf16[256,2560]{1,0:T(8,128)(2,1)S(1)} %copy-done.3, bf16[256,512]{1,0:T(8,128)(2,1)S(1)} %get-tuple-element.17.scaled), custom_call_target="tpu_custom_call" | custom-call | tf_op jit(solution)/shard_map/pallas_call | solution.py:104
  109.3 0.0 reduce-scatter.2.cloned.1.call-update
  109.4 0.0 copy-start.5
  109.4 6.8 %all-to-all-start.1 = ((bf16[8,336,256]{2,1,0:T(8,128)(2,1)}), bf16[8,336,256]{2,1,0:T(8,128)(2,1)S(1)}, u32[]{:S(2)}, u32[]{:S(2)}) async-start(bf16[8,336,256]{2,1,0:T(8,128)(2,1)} %get-tuple-element.14), calls=%async_computation.1 | async-start | bytes 2752512 | tf_op jit(solution)/shard_map/all_to_all | solution.py:137
  116.1 0.0 copy-done.5
  116.2 0.9 shard_map.94
  117.1 19.1 %all-to-all-done.1.refs_0_ = bf16[8,336,256]{2,1,0:T(8,128)(2,1)S(1)} async-done(((bf16[8,336,256]{2,1,0:T(8,128)(2,1)}), bf16[8,336,256]{2,1,0:T(8,128)(2,1)S(1)}, u32[]{:S(2)}, u32[]{:S(2)}) %all-to-all-start.1) | async-done | bytes 1376288 | tf_op jit(solution)/shard_map/all_to_all | solution.py:137
  136.1 0.8 shard_map.96
  137.0 0.0 reduce-scatter.2.cloned.1.call-done
Async XLA Ops:
  7.2 129.8 %reduce-scatter.2.cloned.1.call-start = ((), (), s32[]{:S(2)}) async-start(), calls=%async_computation.3 | async-start | bytes 3932160 | tf_op jit(solution)/shard_map/reduce_scatter | solution.py:139
  7.2 1.7 %copy-start = (bf16[1,2560,512]{2,1,0:T(8,128)(2,1)S(1)}, bf16[1,2560,512]{2,1,0:T(8,128)(2,1)}, u32[]{:S(2)}) copy-start(bf16[1,2560,512]{2,1,0:T(8,128)(2,1)} %param.10) | copy-start | bytes 7864324
  9.0 1.3 copy-start.2
  10.3 0.9 copy-start.4
  11.2 0.7 copy-start.6
  11.9 0.7 copy-start.8
  12.5 92.0 %copy-start.1 = (bf16[1,2560,512]{2,1,0:T(8,128)(2,1)S(1)}, bf16[1,2560,512]{2,1,0:T(8,128)(2,1)}, u32[]{:S(2)}) copy-start(bf16[1,2560,512]{2,1,0:T(8,128)(2,1)} %param.10) | copy-start | bytes 7864324
  12.5 92.0 %copy-start.7 = (f32[256]{0:T(256)S(1)}, f32[256]{0:T(256)}, u32[]{:S(2)}) copy-start(f32[256]{0:T(256)} %param.9) | copy-start | bytes 3076
  104.5 2.4 %copy-start.3 = (bf16[256,2560]{1,0:T(8,128)(2,1)S(1)}, bf16[256,2560]{1,0:T(8,128)(2,1)}, u32[]{:S(2)}) copy-start(bf16[256,2560]{1,0:T(8,128)(2,1)} %hidden.1) | copy-start | bytes 3932164
  109.4 6.8 %copy-start.5 = (bf16[128,512]{1,0:T(8,128)(2,1)S(1)}, bf16[128,512]{1,0:T(8,128)(2,1)}, u32[]{:S(2)}) copy-start(bf16[128,512]{1,0:T(8,128)(2,1)} %residual.1) | copy-start | bytes 393220
  109.4 26.8 %all-to-all-start.1 = ((bf16[8,336,256]{2,1,0:T(8,128)(2,1)}), bf16[8,336,256]{2,1,0:T(8,128)(2,1)S(1)}, u32[]{:S(2)}, u32[]{:S(2)}) async-start(bf16[8,336,256]{2,1,0:T(8,128)(2,1)} %get-tuple-element.14), calls=%async_computation.1 | async-start | bytes 2752512 | tf_op jit(solution)/shard_map/all_to_all | solution.py:137
Sparse Core Ops, SparseCore 0:
  109.5 15.8 reduce-scatter.1

commit v2 on v1

v2 whole, which is shorter than its diff:
```python
import functools

import jax
import jax.numpy as jnp
from jax import lax
from jax.experimental import pallas as pl
from jax.experimental.pallas import tpu as pltpu
from jax.sharding import PartitionSpec as P

F32 = jnp.float32
BF16 = jnp.bfloat16
EXTRA = 16
NEAR = jax.ShapeDtypeStruct


def iota(shape, dim):
    return lax.broadcasted_iota(jnp.int32, shape, dim)


def column_of(row):
    n = row.shape[1]
    same = iota((n, n), 0) == iota((n, n), 1)
    return jnp.sum(jnp.where(same, jnp.broadcast_to(row, (n, n)), 0.0), axis=1, keepdims=True)


def one_hot(mask):
    return mask.astype(F32).astype(BF16)


def dot(a, b, over=((1,), (0,))):
    return lax.dot_general(a, b, (over, ((), ())), preferred_element_type=F32)


def fetch(sources, targets, sems):
    copies = [pltpu.make_async_copy(s, t, sems.at[i]) for i, (s, t) in enumerate(zip(sources, targets))]
    for copy in copies:
        copy.start()
    return copies


def row_slots(slots, per, answers):
    row, slot = iota((2 * slots, slots), 0), iota((2 * slots, slots), 1)
    return one_hot(slot // per * (2 * per) + per * answers + slot % per == row)


def slot_rows(slots, per, answers):
    slot, row = iota((slots, 2 * slots), 0), iota((slots, 2 * slots), 1)
    return one_hot(slot // per * (2 * per) + per * answers + slot % per == row)


def send_kernel(
    per, ids_at, cotangent_at, hidden_at, weight_at, gates_at,
    message, hits, projected, ids, cotangent, hidden, weight, gates, sems,
):
    steps, slots, step = hidden.shape
    sources, targets = [ids_at, cotangent_at, gates_at], [ids, cotangent, gates]
    for k in range(steps):
        sources += [hidden_at.at[:, k * step : (k + 1) * step], weight_at.at[k * step : (k + 1) * step, :]]
        targets += [hidden.at[k], weight.at[k]]
    copies = fetch(sources, targets, sems)
    tokens = ids.shape[1]
    slot = iota((slots, tokens), 0)
    earlier = one_hot(iota((tokens, tokens), 0) < iota((tokens, tokens), 1))
    copies[0].wait()
    named = jnp.logical_or(ids[0:1, :] == slot // per, ids[1:2, :] == slot // per)
    rank = dot(one_hot(named), earlier).astype(jnp.int32)
    table = one_hot(jnp.logical_and(named, rank == slot % per))
    hits[...] = table
    copies[1].wait()
    rows = dot(row_slots(slots, per, 0), dot(table, cotangent[...]).astype(BF16))
    answers = row_slots(slots, per, 1)
    copies[2].wait()
    gate = column_of(gates[...])
    product = None
    for k in range(steps):
        copies[3 + 2 * k].wait()
        copies[4 + 2 * k].wait()
        term = dot(hidden[k], weight[k])
        product = term if product is None else product + term
    projected[...] = product
    message[...] = (rows + dot(answers, (gate * product).astype(BF16))).astype(BF16)


def hidden_kernel(per, parts, arrived, weight, gates, projected, scaled, partial_at, partial, sems):
    slots = scaled.shape[0]
    gate = column_of(gates[...])
    slot_grad = dot(slot_rows(slots, per, 0), arrived[...])
    grown = (gate * slot_grad).astype(BF16)
    scaled[...] = grown
    block = weight.shape[0] // parts
    copies = []
    for part in range(parts):
        partial[part, :block, :] = dot(weight[part * block : (part + 1) * block, :], grown, ((1,), (1,))).astype(BF16)
        copies += fetch(
            [partial.at[part, pl.ds(0, block)]], [partial_at.at[part, pl.ds(0, block)]], sems.at[pl.ds(part, 1)]
        )
    terms = jnp.sum(slot_grad * projected[...], axis=1, keepdims=True).astype(BF16).astype(F32)
    width = slots // parts
    chosen = one_hot(iota((parts, slots), 1) // width == iota((parts, slots), 0))
    lanes = jnp.where(iota((slots, slots), 0) % width == iota((slots, slots), 1), terms, 0.0).astype(BF16)
    gate_rows = dot(chosen, lanes)
    for part in range(parts):
        tail = jnp.where(iota((EXTRA, slots), 0) == 0, gate_rows[part : part + 1, :], 0.0)
        partial[part, block:, :] = tail.astype(BF16)
    copies += fetch(
        [partial.at[:, pl.ds(block, EXTRA)]], [partial_at.at[:, pl.ds(block, EXTRA)]], sems.at[pl.ds(parts, 1)]
    )
    for copy in copies:
        copy.wait()


def columns_of(hidden, part):
    width = hidden.shape[1] // 2
    return hidden[:, pl.ds(pl.multiple_of(part * width, 128), width)]


def weight_give_kernel(hidden, scaled, out):
    part = 1 - lax.axis_index("dp")
    out[...] = dot(columns_of(hidden, part), scaled[...], ((0,), (0,))).astype(BF16)


def weight_keep_kernel(hidden, scaled, got, out):
    part = lax.axis_index("dp")
    out[...] = (dot(columns_of(hidden, part), scaled[...], ((0,), (0,))) + got[...].astype(F32)).astype(BF16)


def combine_kernel(per, arrived, hits, residual, out):
    answers = dot(slot_rows(hits.shape[0], per, 1), arrived[...]).astype(BF16)
    out[...] = (residual[...].astype(F32) + dot(hits[...], answers, ((0,), (0,)))).astype(BF16)


def sum_kernel(parts, partial, weight_grad_at, hidden_grad, gate_grad):
    block, width = hidden_grad.shape[0], gate_grad.shape[1]
    total = partial[0, :block, :].astype(F32)
    gate = partial[0, block:, :].astype(F32)
    for part in range(1, parts):
        total += partial[part, :block, :].astype(F32)
        gate += partial[part, block:, :].astype(F32)
    hidden_grad[...] = total.astype(BF16)
    gate_grad[...] = gate[0:1, :width]


def call(kernel, sizes, outs, *args, far=0, scratch=()):
    near = len(args) - far
    args = args[:near] + tuple(pltpu.with_memory_space_constraint(arg, pltpu.HBM) for arg in args[near:])
    return pl.pallas_call(
        functools.partial(kernel, *sizes),
        out_shape=outs,
        in_specs=[pl.BlockSpec(memory_space=pltpu.VMEM)] * near + [pl.BlockSpec(memory_space=pltpu.HBM)] * far,
        out_specs=[
            pl.BlockSpec(memory_space=pltpu.VMEM if isinstance(out, NEAR) else pltpu.HBM) for out in outs
        ],
        scratch_shapes=list(scratch),
        compiler_params=pltpu.CompilerParams(vmem_limit_bytes=40 * 1024 * 1024),
    )(*args)


def on_device(residual, route_ids, slot_hidden, slot_gates, down_weight, cotangent):
    tokens, width = residual.shape
    experts, parts = lax.axis_size("expert"), lax.axis_size("tensor")
    slots, inner = slot_hidden.shape
    per = slots // experts
    weight = down_weight[0]
    gates = slot_gates[None, :]
    steps = inner // 512
    step = inner // steps

    message, hits, projected = call(
        send_kernel, (per,),
        [NEAR((2 * slots, width), BF16), NEAR((slots, tokens), BF16), NEAR((slots, width), F32)],
        route_ids.T, cotangent, slot_hidden, weight, gates, far=5,
        scratch=[
            pltpu.VMEM((2, tokens), jnp.int32), pltpu.VMEM((tokens, width), BF16),
            pltpu.VMEM((steps, slots, step), BF16), pltpu.VMEM((steps, step, width), BF16),
            pltpu.VMEM((1, slots), F32), pltpu.SemaphoreType.DMA((2 * steps + 3,)),
        ],
    )
    arrived = lax.all_to_all(
        message.reshape(experts, 2 * per, width), "expert", split_axis=0, concat_axis=0, tiled=True
    ).reshape(2 * slots, width)
    scaled, partial = call(
        hidden_kernel, (per, parts),
        [NEAR((slots, width), BF16), pltpu.HBM((parts, inner // parts + EXTRA, slots), BF16)],
        arrived, weight, gates, projected,
        scratch=[
            pltpu.VMEM((parts, inner // parts + EXTRA, slots), BF16), pltpu.SemaphoreType.DMA((parts + 1,)),
        ],
    )
    partial = lax.all_to_all(partial, "tensor", split_axis=0, concat_axis=0, tiled=True)
    (weight_give,) = call(weight_give_kernel, (), [NEAR((inner // 2, width), BF16)], slot_hidden, scaled)
    weight_got = lax.ppermute(weight_give, "dp", [(0, 1), (1, 0)])
    (weight_grad,) = call(
        weight_keep_kernel, (), [NEAR((inner // 2, width), BF16)], slot_hidden, scaled, weight_got
    )
    (combined,) = call(combine_kernel, (per,), [NEAR((tokens, width), BF16)], arrived, hits, residual)
    hidden_grad, gate_grad = call(
        sum_kernel, (parts,), [NEAR((inner // parts, slots), BF16), NEAR((1, slots // parts), F32)],
        partial, weight_grad, far=1,
    )
    return combined, hidden_grad.T, gate_grad[0], weight_grad[None]


def solution(mesh):
    placed = (
        P(("dp", "expert"), "tensor"),
        P(("dp", "expert"), None),
        P(("dp", "expert"), None),
        P(("dp", "expert")),
        P("expert", None, "tensor"),
        P(("dp", "expert"), "tensor"),
    )
    return jax.shard_map(
        on_device,
        mesh=mesh,
        in_specs=placed,
        out_specs=(
            P(("dp", "expert"), "tensor"),
            P(("dp", "expert"), "tensor"),
            P(("dp", "expert", "tensor")),
            P("expert", "dp", "tensor"),
        ),
        check_vma=False,
    )
```

time: 144 us -> 129 us (0.90)
  the two profiles are of different devices: /device:TPU:96 before, /device:TPU:1 now
where the time goes in v2:
time: 129 us; the launch traced here: 127 us
  blocking collectives  86.6 us (67%)
  waiting for transfers between devices  15.6 us (12%)
  Pallas kernels  11.6 us (9%)
  starting transfers between devices  11.3 us (9%)
    all_to_all x1, blocking collectives, on_device(): lax.all_to_all(message.reshape(experts, 2 * per, width), 'expert', split_...  86.6 us
    all_to_all x1, waiting for transfers between devices, on_device(): lax.all_to_all(partial, 'tensor', split_axis=0, concat_axis=0, tiled=True)  15.6 us
    pallas_call x6, Pallas kernels, call(): pl.pallas_call(functools.partial(kernel, *sizes), out_shape=outs, in_spec...  11.6 us
    all_to_all x1, starting transfers between devices, on_device(): lax.all_to_all(partial, 'tensor', split_axis=0, concat_axis=0, tiled=True)  6.37 us
    ppermute x1, starting transfers between devices, on_device(): weight_got = lax.ppermute(weight_give, 'dp', [(0, 1), (1, 0)])  4.97 us
  transfers between devices with their start and end apart: 2, of which 1 were waited for; matrix products, arithmetic and copies ran while one was open for 0% of the time, Pallas kernels for 3%

profile of v2, /device:TPU:1, one launch (start us, length us, event | category | flops | bytes accessed | tf_op | source)
XLA Modules:
  0.0 126.7 jit_solution(9029195152449942242)
XLA Ops:
  0.6 0.0 copy-start.1
  0.6 0.0 copy-start.3
  0.7 3.1 %shard_map.93 = (bf16[512,512]{1,0:T(8,128)(2,1)S(1)}, bf16[256,128]{1,0:T(8,128)(2,1)S(1)}, f32[256,512]{1,0:T(8,128)S(1)}) custom-call(s32[2,128]{1,0:T(2,128)} %bitcast.16, bf16[128,512]{1,0:T(8,128)(2,1)} %cotangent_at.1, bf16[256,2560]{1,0:T(8,128)(2,1)} %hidden.3, bf16[2560,512]{1,0:T(8,128)(2,1)} %bitcast.8, f32[1,256]{1,0:T(1,128)} %bitcast.13), custom_call_target="tpu_custom_call" | custom-call | tf_op jit(solution)/shard_map/pallas_call | solution.py:146
  3.8 86.6 %all_to_all.10 = bf16[64,8,512]{2,1,0:T(8,128)(2,1)S(1)} all-to-all(bf16[64,8,512]{2,1,0:T(8,128)(2,1)S(1)} %bitcast.12), channel_id=1, replica_groups=mesh['dp'=2,'expert'=64,'tensor'=8] {'expert'}, dimensions={0} | all-to-all | bytes 1048576 | tf_op jit(solution)/shard_map/all_to_all | solution.py:178
  90.4 0.0 copy-done.1
  90.4 0.0 copy-done.3
  90.4 0.0 copy-start
  90.4 2.0 %shard_map.95 = (bf16[256,512]{1,0:T(8,128)(2,1)S(1)}, bf16[8,336,256]{2,1,0:T(8,128)(2,1)}) custom-call(bf16[512,512]{1,0:T(8,128)(2,1)S(1)} %bitcast.10, bf16[2560,512]{1,0:T(8,128)(2,1)S(1)} %bitcast.9, f32[1,256]{1,0:T(1,128)S(1)} %bitcast.14, f32[256,512]{1,0:T(8,128)S(1)} %get-tuple-element.13.projected), custom_call_target="tpu_custom_call" | custom-call | tf_op jit(solution)/shard_map/pallas_call | solution.py:146
  92.4 0.0 copy-done
  92.4 1.6 %shard_map.96 = bf16[1280,512]{1,0:T(8,128)(2,1)} custom-call(bf16[256,2560]{1,0:T(8,128)(2,1)S(1)} %copy-done, bf16[256,512]{1,0:T(8,128)(2,1)S(1)} %get-tuple-element.15.scaled), custom_call_target="tpu_custom_call" | custom-call | tf_op jit(solution)/shard_map/pallas_call | solution.py:146
  94.0 5.0 %collective-permute-start = (bf16[1280,512]{1,0:T(8,128)(2,1)}, bf16[1280,512]{1,0:T(8,128)(2,1)}, u32[]{:S(2)}, u32[]{:S(2)}) collective-permute-start(bf16[1280,512]{1,0:T(8,128)(2,1)} %shard_map.96), channel_id=1, source_target_pairs={{0,512},{512,0},{1,513},{513,1},{2,514},{514,2},{3,515},{515,3},{4... | collective-permute-start | bytes 3932168 | tf_op jit(solution)/shard_map/ppermute | solution.py:191
  99.0 6.4 %all-to-all-start.1 = ((bf16[8,336,256]{2,1,0:T(8,128)(2,1)}), bf16[8,336,256]{2,1,0:T(8,128)(2,1)S(1)}, u32[]{:S(2)}, u32[]{:S(2)}) async-start(bf16[8,336,256]{2,1,0:T(8,128)(2,1)} %get-tuple-element.14), calls=%async_computation.1 | async-start | bytes 2752512 | tf_op jit(solution)/shard_map/all_to_all | solution.py:189
  105.3 0.0 copy-start.2
  105.4 0.9 copy-done.2
  106.3 1.1 shard_map.94
  107.4 0.0 collective-permute-done.got
  107.4 2.9 %shard_map.97.weight_grad_at = bf16[1280,512]{1,0:T(8,128)(2,1)} custom-call(bf16[256,2560]{1,0:T(8,128)(2,1)S(1)} %copy-done, bf16[256,512]{1,0:T(8,128)(2,1)S(1)} %get-tuple-element.15.scaled, bf16[1280,512]{1,0:T(8,128)(2,1)} %collective-permute-done.got), custom_call_target="tpu_custom_call" | custom-call | tf_op jit(solution)/shard_map/pallas_call | solution.py:146
  110.3 15.6 %all-to-all-done.1.partial = bf16[8,336,256]{2,1,0:T(8,128)(2,1)S(1)} async-done(((bf16[8,336,256]{2,1,0:T(8,128)(2,1)}), bf16[8,336,256]{2,1,0:T(8,128)(2,1)S(1)}, u32[]{:S(2)}, u32[]{:S(2)}) %all-to-all-start.1) | async-done | bytes 1376288 | tf_op jit(solution)/shard_map/all_to_all | solution.py:189
  125.9 0.8 shard_map.98
Async XLA Ops:
  0.6 89.7 %copy-start.1 = (bf16[1,2560,512]{2,1,0:T(8,128)(2,1)S(1)}, bf16[1,2560,512]{2,1,0:T(8,128)(2,1)}, u32[]{:S(2)}) copy-start(bf16[1,2560,512]{2,1,0:T(8,128)(2,1)} %param.10) | copy-start | bytes 7864324
  0.6 89.7 %copy-start.3 = (f32[256]{0:T(256)S(1)}, f32[256]{0:T(256)}, u32[]{:S(2)}) copy-start(f32[256]{0:T(256)} %param.9) | copy-start | bytes 3076
  90.4 2.0 %copy-start = (bf16[256,2560]{1,0:T(8,128)(2,1)S(1)}, bf16[256,2560]{1,0:T(8,128)(2,1)}, u32[]{:S(2)}) copy-start(bf16[256,2560]{1,0:T(8,128)(2,1)} %hidden.3) | copy-start | bytes 3932164
  94.0 13.4 %collective-permute-start = (bf16[1280,512]{1,0:T(8,128)(2,1)}, bf16[1280,512]{1,0:T(8,128)(2,1)}, u32[]{:S(2)}, u32[]{:S(2)}) collective-permute-start(bf16[1280,512]{1,0:T(8,128)(2,1)} %shard_map.96), channel_id=1, source_target_pairs={{0,512},{512,0},{1,513},{513,1},{2,514},{514,2},{3,515},{515,3},{4... | collective-permute-start | bytes 3932168 | tf_op jit(solution)/shard_map/ppermute | solution.py:191
  99.0 26.9 %all-to-all-start.1 = ((bf16[8,336,256]{2,1,0:T(8,128)(2,1)}), bf16[8,336,256]{2,1,0:T(8,128)(2,1)S(1)}, u32[]{:S(2)}, u32[]{:S(2)}) async-start(bf16[8,336,256]{2,1,0:T(8,128)(2,1)} %get-tuple-element.14), calls=%async_computation.1 | async-start | bytes 2752512 | tf_op jit(solution)/shard_map/all_to_all | solution.py:189
  105.3 0.9 copy-start.2

commit v3 on v2

--- a/solution.py
+++ b/solution.py
@@ -49,14 +49,15 @@
 
 
 def send_kernel(
-    per, ids_at, cotangent_at, hidden_at, weight_at, gates_at,
-    message, hits, projected, ids, cotangent, hidden, weight, gates, sems,
+    per, step, ids_at, cotangent_at, hidden_at, weight_at, gates_at,
+    message, hits, projected, hidden, weight, ids, cotangent, gates, sems,
 ):
-    steps, slots, step = hidden.shape
+    slots, inner = hidden.shape
     sources, targets = [ids_at, cotangent_at, gates_at], [ids, cotangent, gates]
-    for k in range(steps):
-        sources += [hidden_at.at[:, k * step : (k + 1) * step], weight_at.at[k * step : (k + 1) * step, :]]
-        targets += [hidden.at[k], weight.at[k]]
+    spans = [pl.ds(begin, step) for begin in range(0, inner, step)]
+    for span in spans:
+        sources += [hidden_at.at[:, span], weight_at.at[span]]
+        targets += [hidden.at[:, span], weight.at[span]]
     copies = fetch(sources, targets, sems)
     tokens = ids.shape[1]
     slot = iota((slots, tokens), 0)
@@ -72,10 +73,10 @@
     copies[2].wait()
     gate = column_of(gates[...])
     product = None
-    for k in range(steps):
+    for k, span in enumerate(spans):
         copies[3 + 2 * k].wait()
         copies[4 + 2 * k].wait()
-        term = dot(hidden[k], weight[k])
+        term = dot(hidden[:, span], weight[span, :])
         product = term if product is None else product + term
     projected[...] = product
     message[...] = (rows + dot(answers, (gate * product).astype(BF16))).astype(BF16)
@@ -87,24 +88,18 @@
     slot_grad = dot(slot_rows(slots, per, 0), arrived[...])
     grown = (gate * slot_grad).astype(BF16)
     scaled[...] = grown
-    block = weight.shape[0] // parts
-    copies = []
-    for part in range(parts):
-        partial[part, :block, :] = dot(weight[part * block : (part + 1) * block, :], grown, ((1,), (1,))).astype(BF16)
-        copies += fetch(
-            [partial.at[part, pl.ds(0, block)]], [partial_at.at[part, pl.ds(0, block)]], sems.at[pl.ds(part, 1)]
-        )
     terms = jnp.sum(slot_grad * projected[...], axis=1, keepdims=True).astype(BF16).astype(F32)
     width = slots // parts
     chosen = one_hot(iota((parts, slots), 1) // width == iota((parts, slots), 0))
     lanes = jnp.where(iota((slots, slots), 0) % width == iota((slots, slots), 1), terms, 0.0).astype(BF16)
     gate_rows = dot(chosen, lanes)
+    block = weight.shape[0] // parts
+    copies = []
     for part in range(parts):
         tail = jnp.where(iota((EXTRA, slots), 0) == 0, gate_rows[part : part + 1, :], 0.0)
         partial[part, block:, :] = tail.astype(BF16)
-    copies += fetch(
-        [partial.at[:, pl.ds(block, EXTRA)]], [partial_at.at[:, pl.ds(block, EXTRA)]], sems.at[pl.ds(parts, 1)]
-    )
+        partial[part, :block, :] = dot(weight[part * block : (part + 1) * block, :], grown, ((1,), (1,))).astype(BF16)
+        copies += fetch([partial.at[part]], [partial_at.at[part]], sems.at[pl.ds(part, 1)])
     for copy in copies:
         copy.wait()
 
@@ -114,14 +109,18 @@
     return hidden[:, pl.ds(pl.multiple_of(part * width, 128), width)]
 
 
-def weight_give_kernel(hidden, scaled, out):
-    part = 1 - lax.axis_index("dp")
-    out[...] = dot(columns_of(hidden, part), scaled[...], ((0,), (0,))).astype(BF16)
-
-
-def weight_keep_kernel(hidden, scaled, got, out):
-    part = lax.axis_index("dp")
-    out[...] = (dot(columns_of(hidden, part), scaled[...], ((0,), (0,))) + got[...].astype(F32)).astype(BF16)
+def weight_give_kernel(hidden, scaled, first, second):
+    product = dot(columns_of(hidden, 1 - lax.axis_index("dp")), scaled[...], ((0,), (0,))).astype(BF16)
+    half = first.shape[0]
+    first[...] = product[:half]
+    second[...] = product[half:]
+
+
+def weight_keep_kernel(hidden, scaled, first, second, out):
+    product = dot(columns_of(hidden, lax.axis_index("dp")), scaled[...], ((0,), (0,)))
+    half = first.shape[0]
+    out[:half, :] = (product[:half] + first[...].astype(F32)).astype(BF16)
+    out[half:, :] = (product[half:] + second[...].astype(F32)).astype(BF16)
 
 
 def combine_kernel(per, arrived, hits, residual, out):
@@ -148,7 +147,7 @@
         out_shape=outs,
         in_specs=[pl.BlockSpec(memory_space=pltpu.VMEM)] * near + [pl.BlockSpec(memory_space=pltpu.HBM)] * far,
         out_specs=[
-            pl.BlockSpec(memory_space=pltpu.VMEM if isinstance(out, NEAR) else pltpu.HBM) for out in outs
+            pl.BlockSpec(memory_space=pltpu.VMEM if isinstance(out, NEAR) else out.memory_space) for out in outs
         ],
         scratch_shapes=list(scratch),
         compiler_params=pltpu.CompilerParams(vmem_limit_bytes=40 * 1024 * 1024),
@@ -160,19 +159,19 @@
     experts, parts = lax.axis_size("expert"), lax.axis_size("tensor")
     slots, inner = slot_hidden.shape
     per = slots // experts
-    weight = down_weight[0]
     gates = slot_gates[None, :]
-    steps = inner // 512
-    step = inner // steps
-
-    message, hits, projected = call(
-        send_kernel, (per,),
-        [NEAR((2 * slots, width), BF16), NEAR((slots, tokens), BF16), NEAR((slots, width), F32)],
-        route_ids.T, cotangent, slot_hidden, weight, gates, far=5,
+    step = 512
+
+    message, hits, projected, hidden, weight = call(
+        send_kernel, (per, step),
+        [
+            NEAR((2 * slots, width), BF16), NEAR((slots, tokens), BF16), NEAR((slots, width), F32),
+            pltpu.VMEM((slots, inner), BF16), pltpu.VMEM((inner, width), BF16),
+        ],
+        route_ids.T, cotangent, slot_hidden, down_weight[0], gates, far=5,
         scratch=[
             pltpu.VMEM((2, tokens), jnp.int32), pltpu.VMEM((tokens, width), BF16),
-            pltpu.VMEM((steps, slots, step), BF16), pltpu.VMEM((steps, step, width), BF16),
-            pltpu.VMEM((1, slots), F32), pltpu.SemaphoreType.DMA((2 * steps + 3,)),
+            pltpu.VMEM((1, slots), F32), pltpu.SemaphoreType.DMA((2 * (inner // step) + 3,)),
         ],
     )
     arrived = lax.all_to_all(
@@ -183,14 +182,14 @@
         [NEAR((slots, width), BF16), pltpu.HBM((parts, inner // parts + EXTRA, slots), BF16)],
         arrived, weight, gates, projected,
         scratch=[
-            pltpu.VMEM((parts, inner // parts + EXTRA, slots), BF16), pltpu.SemaphoreType.DMA((parts + 1,)),
+            pltpu.VMEM((parts, inner // parts + EXTRA, slots), BF16), pltpu.SemaphoreType.DMA((parts,)),
         ],
     )
     partial = lax.all_to_all(partial, "tensor", split_axis=0, concat_axis=0, tiled=True)
-    (weight_give,) = call(weight_give_kernel, (), [NEAR((inner // 2, width), BF16)], slot_hidden, scaled)
-    weight_got = lax.ppermute(weight_give, "dp", [(0, 1), (1, 0)])
+    weight_give = call(weight_give_kernel, (), [NEAR((inner // 4, width), BF16)] * 2, hidden, scaled)
+    weight_got = [lax.ppermute(part, "dp", [(0, 1), (1, 0)]) for part in weight_give]
     (weight_grad,) = call(
-        weight_keep_kernel, (), [NEAR((inner // 2, width), BF16)], slot_hidden, scaled, weight_got
+        weight_keep_kernel, (), [NEAR((inner // 2, width), BF16)], hidden, scaled, *weight_got
     )
     (combined,) = call(combine_kernel, (per,), [NEAR((tokens, width), BF16)], arrived, hits, residual)
     hidden_grad, gate_grad = call(

time: 129 us -> 124 us (0.961)
  the two profiles are of different devices: /device:TPU:1 before, /device:TPU:96 now
where the time goes in v3:
time: 124 us
  blocking collectives  90.6 us (73%)
  waiting for transfers between devices  12.4 us (10%)
  starting transfers between devices  11 us (9%)
  Pallas kernels  9.26 us (7%)
    all_to_all x1, blocking collectives, on_device(): lax.all_to_all(message.reshape(experts, 2 * per, width), 'expert', split_...  90.6 us
    all_to_all x1, waiting for transfers between devices, on_device(): lax.all_to_all(partial, 'tensor', split_axis=0, concat_axis=0, tiled=True)  11.8 us
    pallas_call x6, Pallas kernels, call(): pl.pallas_call(functools.partial(kernel, *sizes), out_shape=outs, in_spec...  9.26 us
    all_to_all x1, starting transfers between devices, on_device(): lax.all_to_all(partial, 'tensor', split_axis=0, concat_axis=0, tiled=True)  6.66 us
    ppermute x2, starting transfers between devices, on_device(): lax.ppermute(part, 'dp', [(0, 1), (1, 0)])  4.33 us
  transfers between devices with their start and end apart: 3, of which 2 were waited for; matrix products, arithmetic and copies ran while one was open for 0% of the time, Pallas kernels for 3%

profile of v3, /device:TPU:96, one launch (start us, length us, event | category | flops | bytes accessed | tf_op | source)
XLA Modules:
  0.0 124.0 jit_solution(10610943709511722909)
XLA Ops:
  0.6 0.0 copy-start.1
  0.6 3.0 %shard_map.93 = (bf16[512,512]{1,0:T(8,128)(2,1)S(1)}, bf16[256,128]{1,0:T(8,128)(2,1)S(1)}, f32[256,512]{1,0:T(8,128)S(1)}, bf16[256,2560]{1,0:T(8,128)(2,1)S(1)}, bf16[2560,512]{1,0:T(8,128)(2,1)S(1)}) custom-call(s32[2,128]{1,0:T(2,128)} %bitcast.15, bf16[128,512]{1,0:T(8,128)(2,1)} %cotangent_at.1, bf16[256,2560]{1,0:T(8,128)(2,1)} %hidden_at.1, ...), custom_call_target="tpu_custom_call" | custom-call | tf_op jit(solution)/shard_map/pallas_call | solution.py:145
  3.7 90.6 %all_to_all.10 = bf16[64,8,512]{2,1,0:T(8,128)(2,1)S(1)} all-to-all(bf16[64,8,512]{2,1,0:T(8,128)(2,1)S(1)} %bitcast.10), channel_id=1, replica_groups=mesh['dp'=2,'expert'=64,'tensor'=8] {'expert'}, dimensions={0} | all-to-all | bytes 1048576 | tf_op jit(solution)/shard_map/all_to_all | solution.py:177
  94.3 0.0 copy-done.1
  94.3 2.2 %shard_map.95 = (bf16[256,512]{1,0:T(8,128)(2,1)S(1)}, bf16[8,336,256]{2,1,0:T(8,128)(2,1)}) custom-call(bf16[512,512]{1,0:T(8,128)(2,1)S(1)} %bitcast.8, bf16[2560,512]{1,0:T(8,128)(2,1)S(1)} %get-tuple-element.17.weight, f32[1,256]{1,0:T(1,128)S(1)} %bitcast.12, f32[256,512]{1,0:T(8,128)S(1)} %get-tuple-element.18.projected), custom_call_target="tpu_custom_call" | custom-call | tf_op jit(solution)/shard_map/pallas_call | solution.py:145
  96.5 6.7 %all-to-all-start.1 = ((bf16[8,336,256]{2,1,0:T(8,128)(2,1)}), bf16[8,336,256]{2,1,0:T(8,128)(2,1)S(1)}, u32[]{:S(2)}, u32[]{:S(2)}) async-start(bf16[8,336,256]{2,1,0:T(8,128)(2,1)} %get-tuple-element.19), calls=%async_computation.1 | async-start | bytes 2752512 | tf_op jit(solution)/shard_map/all_to_all | solution.py:188
  103.1 0.0 copy-start
  103.1 0.5 shard_map.96
  103.7 1.9 %collective-permute-start = (bf16[640,512]{1,0:T(8,128)(2,1)S(1)}, bf16[640,512]{1,0:T(8,128)(2,1)S(1)}, u32[]{:S(2)}, u32[]{:S(2)}) collective-permute-start(bf16[640,512]{1,0:T(8,128)(2,1)S(1)} %get-tuple-element.22), channel_id=1, source_target_pairs={{0,512},{512,0},{1,513},{513,1},{2,514},{514,2},{3,515},{515,3},{4... | collective-permute-start | bytes 1966088 | tf_op jit(solution)/shard_map/ppermute | solution.py:190
  105.6 2.4 %collective-permute-start.1 = (bf16[640,512]{1,0:T(8,128)(2,1)S(1)}, bf16[640,512]{1,0:T(8,128)(2,1)S(1)}, u32[]{:S(2)}, u32[]{:S(2)}) collective-permute-start(bf16[640,512]{1,0:T(8,128)(2,1)S(1)} %get-tuple-element.23), channel_id=1, source_target_pairs={{0,512},{512,0},{1,513},{513,1},{2,514},{514,2},{3,515},{515,3},{4... | collective-permute-start | bytes 1966088 | tf_op jit(solution)/shard_map/ppermute | solution.py:190
  108.0 0.0 copy-done
  108.0 1.1 shard_map.94
  109.2 0.0 collective-permute-done.first
  109.2 0.6 collective-permute-done.1.second
  109.7 1.6 %shard_map.97.weight_grad_at = bf16[1280,512]{1,0:T(8,128)(2,1)} custom-call(bf16[256,2560]{1,0:T(8,128)(2,1)S(1)} %get-tuple-element.20.hidden, bf16[256,512]{1,0:T(8,128)(2,1)S(1)} %get-tuple-element.21.scaled, bf16[640,512]{1,0:T(8,128)(2,1)S(1)} %collective-permute-done.first, bf16[640,512]{1,0:T(8,128)(2,1)S(1)} %collective-permute-done.1.second), custom_call_target="tpu_custom_call" | custom-call | tf_op jit(solution)/shard_map/pallas_call | solution.py:145
  111.3 11.8 %all-to-all-done.1.partial = bf16[8,336,256]{2,1,0:T(8,128)(2,1)S(1)} async-done(((bf16[8,336,256]{2,1,0:T(8,128)(2,1)}), bf16[8,336,256]{2,1,0:T(8,128)(2,1)S(1)}, u32[]{:S(2)}, u32[]{:S(2)}) %all-to-all-start.1) | async-done | bytes 1376288 | tf_op jit(solution)/shard_map/all_to_all | solution.py:188
  123.1 0.8 shard_map.98
Async XLA Ops:
  0.6 93.7 %copy-start.1 = (f32[256]{0:T(256)S(1)}, f32[256]{0:T(256)}, u32[]{:S(2)}) copy-start(f32[256]{0:T(256)} %param.9) | copy-start | bytes 3076
  96.5 26.6 %all-to-all-start.1 = ((bf16[8,336,256]{2,1,0:T(8,128)(2,1)}), bf16[8,336,256]{2,1,0:T(8,128)(2,1)S(1)}, u32[]{:S(2)}, u32[]{:S(2)}) async-start(bf16[8,336,256]{2,1,0:T(8,128)(2,1)} %get-tuple-element.19), calls=%async_computation.1 | async-start | bytes 2752512 | tf_op jit(solution)/shard_map/all_to_all | solution.py:188
  103.1 4.9 %copy-start = (bf16[128,512]{1,0:T(8,128)(2,1)S(1)}, bf16[128,512]{1,0:T(8,128)(2,1)}, u32[]{:S(2)}) copy-start(bf16[128,512]{1,0:T(8,128)(2,1)} %residual.1) | copy-start | bytes 393220
  103.7 5.5 %collective-permute-start = (bf16[640,512]{1,0:T(8,128)(2,1)S(1)}, bf16[640,512]{1,0:T(8,128)(2,1)S(1)}, u32[]{:S(2)}, u32[]{:S(2)}) collective-permute-start(bf16[640,512]{1,0:T(8,128)(2,1)S(1)} %get-tuple-element.22), channel_id=1, source_target_pairs={{0,512},{512,0},{1,513},{513,1},{2,514},{514,2},{3,515},{515,3},{4... | collective-permute-start | bytes 1966088 | tf_op jit(solution)/shard_map/ppermute | solution.py:190
  105.6 4.1 %collective-permute-start.1 = (bf16[640,512]{1,0:T(8,128)(2,1)S(1)}, bf16[640,512]{1,0:T(8,128)(2,1)S(1)}, u32[]{:S(2)}, u32[]{:S(2)}) collective-permute-start(bf16[640,512]{1,0:T(8,128)(2,1)S(1)} %get-tuple-element.23), channel_id=1, source_target_pairs={{0,512},{512,0},{1,513},{513,1},{2,514},{514,2},{3,515},{515,3},{4... | collective-permute-start | bytes 1966088 | tf_op jit(solution)/shard_map/ppermute | solution.py:190

commit v4 on v3

--- a/solution.py
+++ b/solution.py
@@ -49,7 +49,7 @@
 
 
 def send_kernel(
-    per, step, ids_at, cotangent_at, hidden_at, weight_at, gates_at,
+    per, step, token, ids_at, cotangent_at, hidden_at, weight_at, gates_at,
     message, hits, projected, hidden, weight, ids, cotangent, gates, sems,
 ):
     slots, inner = hidden.shape
@@ -88,18 +88,22 @@
     slot_grad = dot(slot_rows(slots, per, 0), arrived[...])
     grown = (gate * slot_grad).astype(BF16)
     scaled[...] = grown
+    block = weight.shape[0] // parts
+    copies = []
+    for part in range(parts):
+        partial[part, :block, :] = dot(weight[part * block : (part + 1) * block, :], grown, ((1,), (1,))).astype(BF16)
+        span = part, pl.ds(0, block)
+        copies += fetch([partial.at[span]], [partial_at.at[span]], sems.at[pl.ds(part, 1)])
     terms = jnp.sum(slot_grad * projected[...], axis=1, keepdims=True).astype(BF16).astype(F32)
     width = slots // parts
     chosen = one_hot(iota((parts, slots), 1) // width == iota((parts, slots), 0))
     lanes = jnp.where(iota((slots, slots), 0) % width == iota((slots, slots), 1), terms, 0.0).astype(BF16)
     gate_rows = dot(chosen, lanes)
-    block = weight.shape[0] // parts
-    copies = []
     for part in range(parts):
         tail = jnp.where(iota((EXTRA, slots), 0) == 0, gate_rows[part : part + 1, :], 0.0)
         partial[part, block:, :] = tail.astype(BF16)
-        partial[part, :block, :] = dot(weight[part * block : (part + 1) * block, :], grown, ((1,), (1,))).astype(BF16)
-        copies += fetch([partial.at[part]], [partial_at.at[part]], sems.at[pl.ds(part, 1)])
+    span = slice(None), pl.ds(block, EXTRA)
+    copies += fetch([partial.at[span]], [partial_at.at[span]], sems.at[pl.ds(parts, 1)])
     for copy in copies:
         copy.wait()
 
@@ -162,13 +166,16 @@
     gates = slot_gates[None, :]
     step = 512
 
+    token = lax.ppermute(
+        gates, ("dp", "expert"), [(experts + i, experts + (i + experts // 4) % experts) for i in range(experts)]
+    )
     message, hits, projected, hidden, weight = call(
         send_kernel, (per, step),
         [
             NEAR((2 * slots, width), BF16), NEAR((slots, tokens), BF16), NEAR((slots, width), F32),
             pltpu.VMEM((slots, inner), BF16), pltpu.VMEM((inner, width), BF16),
         ],
-        route_ids.T, cotangent, slot_hidden, down_weight[0], gates, far=5,
+        token, route_ids.T, cotangent, slot_hidden, down_weight[0], gates, far=5,
         scratch=[
             pltpu.VMEM((2, tokens), jnp.int32), pltpu.VMEM((tokens, width), BF16),
             pltpu.VMEM((1, slots), F32), pltpu.SemaphoreType.DMA((2 * (inner // step) + 3,)),
@@ -182,7 +189,7 @@
         [NEAR((slots, width), BF16), pltpu.HBM((parts, inner // parts + EXTRA, slots), BF16)],
         arrived, weight, gates, projected,
         scratch=[
-            pltpu.VMEM((parts, inner // parts + EXTRA, slots), BF16), pltpu.SemaphoreType.DMA((parts,)),
+            pltpu.VMEM((parts, inner // parts + EXTRA, slots), BF16), pltpu.SemaphoreType.DMA((parts + 1,)),
         ],
     )
     partial = lax.all_to_all(partial, "tensor", split_axis=0, concat_axis=0, tiled=True)

time: 124 us -> 121 us (0.976)
  the two profiles are of different devices: /device:TPU:96 before, /device:TPU:1 now
where the time goes in v4:
time: 121 us; the launch traced here: 120 us
  blocking collectives  62.3 us (51%)
  starting transfers between devices  40.2 us (33%)
  Pallas kernels  9.09 us (8%)
  waiting for transfers between devices  8.06 us (7%)
    all_to_all x1, blocking collectives, on_device(): lax.all_to_all(message.reshape(experts, 2 * per, width), 'expert', split_...  62.3 us
    ppermute x1, starting transfers between devices, on_device(): lax.ppermute(gates, ('dp', 'expert'), [(experts + i, experts + (i + exper...  29.5 us
    pallas_call x6, Pallas kernels, call(): pl.pallas_call(functools.partial(kernel, *sizes), out_shape=outs, in_spec...  9.09 us
    all_to_all x1, starting transfers between devices, on_device(): lax.all_to_all(partial, 'tensor', split_axis=0, concat_axis=0, tiled=True)  6.37 us
    all_to_all x1, waiting for transfers between devices, on_device(): lax.all_to_all(partial, 'tensor', split_axis=0, concat_axis=0, tiled=True)  5.4 us
    ppermute x2, starting transfers between devices, on_device(): lax.ppermute(part, 'dp', [(0, 1), (1, 0)])  4.33 us
  transfers between devices with their start and end apart: 4, of which 3 were waited for; matrix products, arithmetic and copies ran while one was open for 0% of the time, Pallas kernels for 3%

profile of v4, /device:TPU:1, one launch (start us, length us, event | category | flops | bytes accessed | tf_op | source)
XLA Modules:
  0.0 120.4 jit_solution(15835052270818389025)
XLA Ops:
  0.6 29.5 %collective-permute-start = (f32[1,256]{1,0:T(1,128)}, f32[1,256]{1,0:T(1,128)S(1)}, u32[]{:S(2)}, u32[]{:S(2)}) collective-permute-start(f32[1,256]{1,0:T(1,128)} %bitcast.11), channel_id=1, source_target_pairs={{512,640},{520,648},{528,656},{536,664},{544,672},{552,680},{560,6... | collective-permute-start | bytes 3080 | tf_op jit(solution)/shard_map/ppermute | solution.py:169
  30.2 2.1 %collective-permute-done.token = f32[1,256]{1,0:T(1,128)S(1)} collective-permute-done((f32[1,256]{1,0:T(1,128)}, f32[1,256]{1,0:T(1,128)S(1)}, u32[]{:S(2)}, u32[]{:S(2)}) %collective-permute-start) | collective-permute-done | bytes 1056 | tf_op jit(solution)/shard_map/ppermute | solution.py:169
  32.2 0.0 copy-start.1
  32.2 3.0 %shard_map.93 = (bf16[512,512]{1,0:T(8,128)(2,1)S(1)}, bf16[256,128]{1,0:T(8,128)(2,1)S(1)}, f32[256,512]{1,0:T(8,128)S(1)}, bf16[256,2560]{1,0:T(8,128)(2,1)S(1)}, bf16[2560,512]{1,0:T(8,128)(2,1)S(1)}) custom-call(f32[1,256]{1,0:T(1,128)S(1)} %collective-permute-done.token, s32[2,128]{1,0:T(2,128)} %bitcast.16, bf16[128,512]{1,0:T(8,128)(2,1)} %cotangent_at.1, ...), custom_call_target="tpu_custom_call" | custom-call | tf_op jit(solution)/shard_map/pallas_call | solution.py:149
  35.3 62.3 %all_to_all.10 = bf16[64,8,512]{2,1,0:T(8,128)(2,1)S(1)} all-to-all(bf16[64,8,512]{2,1,0:T(8,128)(2,1)S(1)} %bitcast.10), channel_id=1, replica_groups=mesh['dp'=2,'expert'=64,'tensor'=8] {'expert'}, dimensions={0} | all-to-all | bytes 1048576 | tf_op jit(solution)/shard_map/all_to_all | solution.py:184
  97.6 0.0 copy-done.1
  97.6 2.0 %shard_map.95 = (bf16[256,512]{1,0:T(8,128)(2,1)S(1)}, bf16[8,336,256]{2,1,0:T(8,128)(2,1)}) custom-call(bf16[512,512]{1,0:T(8,128)(2,1)S(1)} %bitcast.8, bf16[2560,512]{1,0:T(8,128)(2,1)S(1)} %get-tuple-element.17.weight, f32[1,256]{1,0:T(1,128)S(1)} %bitcast.13, f32[256,512]{1,0:T(8,128)S(1)} %get-tuple-element.18.projected), custom_call_target="tpu_custom_call" | custom-call | tf_op jit(solution)/shard_map/pallas_call | solution.py:149
  99.6 6.4 %all-to-all-start.1 = ((bf16[8,336,256]{2,1,0:T(8,128)(2,1)}), bf16[8,336,256]{2,1,0:T(8,128)(2,1)S(1)}, u32[]{:S(2)}, u32[]{:S(2)}) async-start(bf16[8,336,256]{2,1,0:T(8,128)(2,1)} %get-tuple-element.19), calls=%async_computation.1 | async-start | bytes 2752512 | tf_op jit(solution)/shard_map/all_to_all | solution.py:195
  105.9 0.0 copy-start
  106.0 0.5 shard_map.96
  106.5 1.9 %collective-permute-start.1 = (bf16[640,512]{1,0:T(8,128)(2,1)S(1)}, bf16[640,512]{1,0:T(8,128)(2,1)S(1)}, u32[]{:S(2)}, u32[]{:S(2)}) collective-permute-start(bf16[640,512]{1,0:T(8,128)(2,1)S(1)} %get-tuple-element.22), channel_id=1, source_target_pairs={{0,512},{512,0},{1,513},{513,1},{2,514},{514,2},{3,515},{515,3},{4... | collective-permute-start | bytes 1966088 | tf_op jit(solution)/shard_map/ppermute | solution.py:197
  108.4 2.4 %collective-permute-start.2 = (bf16[640,512]{1,0:T(8,128)(2,1)S(1)}, bf16[640,512]{1,0:T(8,128)(2,1)S(1)}, u32[]{:S(2)}, u32[]{:S(2)}) collective-permute-start(bf16[640,512]{1,0:T(8,128)(2,1)S(1)} %get-tuple-element.23), channel_id=1, source_target_pairs={{0,512},{512,0},{1,513},{513,1},{2,514},{514,2},{3,515},{515,3},{4... | collective-permute-start | bytes 1966088 | tf_op jit(solution)/shard_map/ppermute | solution.py:197
  110.8 0.0 copy-done
  110.9 1.1 shard_map.94
  112.0 0.0 collective-permute-done.1.first
  112.0 0.6 collective-permute-done.2.second
  112.5 1.6 %shard_map.97.weight_grad_at = bf16[1280,512]{1,0:T(8,128)(2,1)} custom-call(bf16[256,2560]{1,0:T(8,128)(2,1)S(1)} %get-tuple-element.20.hidden, bf16[256,512]{1,0:T(8,128)(2,1)S(1)} %get-tuple-element.21.scaled, bf16[640,512]{1,0:T(8,128)(2,1)S(1)} %collective-permute-done.1.first, bf16[640,512]{1,0:T(8,128)(2,1)S(1)} %collective-permute-done.2.second), custom_call_target="tpu_custom_call" | custom-call | tf_op jit(solution)/shard_map/pallas_call | solution.py:149
  114.2 5.4 %all-to-all-done.1.partial = bf16[8,336,256]{2,1,0:T(8,128)(2,1)S(1)} async-done(((bf16[8,336,256]{2,1,0:T(8,128)(2,1)}), bf16[8,336,256]{2,1,0:T(8,128)(2,1)S(1)}, u32[]{:S(2)}, u32[]{:S(2)}) %all-to-all-start.1) | async-done | bytes 1376288 | tf_op jit(solution)/shard_map/all_to_all | solution.py:195
  119.6 0.8 shard_map.98
Async XLA Ops:
  0.6 31.6 %collective-permute-start = (f32[1,256]{1,0:T(1,128)}, f32[1,256]{1,0:T(1,128)S(1)}, u32[]{:S(2)}, u32[]{:S(2)}) collective-permute-start(f32[1,256]{1,0:T(1,128)} %bitcast.11), channel_id=1, source_target_pairs={{512,640},{520,648},{528,656},{536,664},{544,672},{552,680},{560,6... | collective-permute-start | bytes 3080 | tf_op jit(solution)/shard_map/ppermute | solution.py:169
  32.2 65.3 %copy-start.1 = (f32[256]{0:T(256)S(1)}, f32[256]{0:T(256)}, u32[]{:S(2)}) copy-start(f32[256]{0:T(256)} %param.9) | copy-start | bytes 3076
  99.6 20.0 %all-to-all-start.1 = ((bf16[8,336,256]{2,1,0:T(8,128)(2,1)}), bf16[8,336,256]{2,1,0:T(8,128)(2,1)S(1)}, u32[]{:S(2)}, u32[]{:S(2)}) async-start(bf16[8,336,256]{2,1,0:T(8,128)(2,1)} %get-tuple-element.19), calls=%async_computation.1 | async-start | bytes 2752512 | tf_op jit(solution)/shard_map/all_to_all | solution.py:195
  105.9 4.9 %copy-start = (bf16[128,512]{1,0:T(8,128)(2,1)S(1)}, bf16[128,512]{1,0:T(8,128)(2,1)}, u32[]{:S(2)}) copy-start(bf16[128,512]{1,0:T(8,128)(2,1)} %residual.1) | copy-start | bytes 393220
  106.5 5.5 %collective-permute-start.1 = (bf16[640,512]{1,0:T(8,128)(2,1)S(1)}, bf16[640,512]{1,0:T(8,128)(2,1)S(1)}, u32[]{:S(2)}, u32[]{:S(2)}) collective-permute-start(bf16[640,512]{1,0:T(8,128)(2,1)S(1)} %get-tuple-element.22), channel_id=1, source_target_pairs={{0,512},{512,0},{1,513},{513,1},{2,514},{514,2},{3,515},{515,3},{4... | collective-permute-start | bytes 1966088 | tf_op jit(solution)/shard_map/ppermute | solution.py:197
  108.4 4.1 %collective-permute-start.2 = (bf16[640,512]{1,0:T(8,128)(2,1)S(1)}, bf16[640,512]{1,0:T(8,128)(2,1)S(1)}, u32[]{:S(2)}, u32[]{:S(2)}) collective-permute-start(bf16[640,512]{1,0:T(8,128)(2,1)S(1)} %get-tuple-element.23), channel_id=1, source_target_pairs={{0,512},{512,0},{1,513},{513,1},{2,514},{514,2},{3,515},{515,3},{4... | collective-permute-start | bytes 1966088 | tf_op jit(solution)/shard_map/ppermute | solution.py:197

commit v5 on v4

--- a/solution.py
+++ b/solution.py
@@ -38,9 +38,23 @@
     return copies
 
 
-def row_slots(slots, per, answers):
-    row, slot = iota((2 * slots, slots), 0), iota((2 * slots, slots), 1)
-    return one_hot(slot // per * (2 * per) + per * answers + slot % per == row)
+def pairs_of(rows):
+    tiles = rows.reshape(-1, 2, 8, rows.shape[1])
+    return tiles[:, 0], tiles[:, 1]
+
+
+def interleave(picks, answers):
+    picks, answers = (x.reshape(-1, 8, x.shape[1]) for x in (picks, answers))
+    low = lax.broadcasted_iota(jnp.int32, picks.shape, 1) < 4
+    even = jnp.where(low, picks, pltpu.roll(answers, 4, 1))
+    odd = jnp.where(low, pltpu.roll(picks, 4, 1), answers)
+    return jnp.stack([even, odd], axis=1).reshape(-1, picks.shape[2])
+
+
+def picks_of(rows):
+    even, odd = pairs_of(rows)
+    low = lax.broadcasted_iota(jnp.int32, even.shape, 1) < 4
+    return jnp.where(low, even, pltpu.roll(odd, 4, 1)).reshape(-1, rows.shape[1])
 
 
 def slot_rows(slots, per, answers):
@@ -68,8 +82,7 @@
     table = one_hot(jnp.logical_and(named, rank == slot % per))
     hits[...] = table
     copies[1].wait()
-    rows = dot(row_slots(slots, per, 0), dot(table, cotangent[...]).astype(BF16))
-    answers = row_slots(slots, per, 1)
+    picks = dot(table, cotangent[...])
     copies[2].wait()
     gate = column_of(gates[...])
     product = None
@@ -79,13 +92,13 @@
         term = dot(hidden[:, span], weight[span, :])
         product = term if product is None else product + term
     projected[...] = product
-    message[...] = (rows + dot(answers, (gate * product).astype(BF16))).astype(BF16)
+    message[...] = interleave(picks, gate * product).astype(BF16)
 
 
 def hidden_kernel(per, parts, arrived, weight, gates, projected, scaled, partial_at, partial, sems):
     slots = scaled.shape[0]
     gate = column_of(gates[...])
-    slot_grad = dot(slot_rows(slots, per, 0), arrived[...])
+    slot_grad = picks_of(arrived[...].astype(F32))
     grown = (gate * slot_grad).astype(BF16)
     scaled[...] = grown
     block = weight.shape[0] // parts
@@ -94,16 +107,17 @@
         partial[part, :block, :] = dot(weight[part * block : (part + 1) * block, :], grown, ((1,), (1,))).astype(BF16)
         span = part, pl.ds(0, block)
         copies += fetch([partial.at[span]], [partial_at.at[span]], sems.at[pl.ds(part, 1)])
-    terms = jnp.sum(slot_grad * projected[...], axis=1, keepdims=True).astype(BF16).astype(F32)
-    width = slots // parts
-    chosen = one_hot(iota((parts, slots), 1) // width == iota((parts, slots), 0))
-    lanes = jnp.where(iota((slots, slots), 0) % width == iota((slots, slots), 1), terms, 0.0).astype(BF16)
-    gate_rows = dot(chosen, lanes)
-    for part in range(parts):
-        tail = jnp.where(iota((EXTRA, slots), 0) == 0, gate_rows[part : part + 1, :], 0.0)
-        partial[part, block:, :] = tail.astype(BF16)
-    span = slice(None), pl.ds(block, EXTRA)
-    copies += fetch([partial.at[span]], [partial_at.at[span]], sems.at[pl.ds(parts, 1)])
+        if part == parts // 2 - 1:
+            terms = jnp.sum(slot_grad * projected[...], axis=1, keepdims=True).astype(BF16).astype(F32)
+            width = slots // parts
+            chosen = one_hot(iota((parts, slots), 1) // width == iota((parts, slots), 0))
+            lanes = jnp.where(iota((slots, slots), 0) % width == iota((slots, slots), 1), terms, 0.0).astype(BF16)
+            gate_rows = dot(chosen, lanes)
+            for at in range(parts):
+                tail = jnp.where(iota((EXTRA, slots), 0) == 0, gate_rows[at : at + 1, :], 0.0)
+                partial[at, block:, :] = tail.astype(BF16)
+            span = slice(None), pl.ds(block, EXTRA)
+            copies += fetch([partial.at[span]], [partial_at.at[span]], sems.at[pl.ds(parts, 1)])
     for copy in copies:
         copy.wait()
 

time: 121 us -> 120 us (level)
  no operation moved by 1% of the time
where the time goes in v5:
time: 120 us
  blocking collectives  62.3 us (52%)
  starting transfers between devices  40.2 us (34%)
  Pallas kernels  8.56 us (7%)
  waiting for transfers between devices  8.05 us (7%)
    all_to_all x1, blocking collectives, on_device(): lax.all_to_all(message.reshape(experts, 2 * per, width), 'expert', split_...  62.3 us
    ppermute x1, starting transfers between devices, on_device(): lax.ppermute(gates, ('dp', 'expert'), [(experts + i, experts + (i + exper...  29.5 us
    pallas_call x6, Pallas kernels, call(): pl.pallas_call(functools.partial(kernel, *sizes), out_shape=outs, in_spec...  8.56 us
    all_to_all x1, starting transfers between devices, on_device(): lax.all_to_all(partial, 'tensor', split_axis=0, concat_axis=0, tiled=True)  6.37 us
    all_to_all x1, waiting for transfers between devices, on_device(): lax.all_to_all(partial, 'tensor', split_axis=0, concat_axis=0, tiled=True)  5.4 us
    ppermute x2, starting transfers between devices, on_device(): lax.ppermute(part, 'dp', [(0, 1), (1, 0)])  4.33 us
  transfers between devices with their start and end apart: 4, of which 3 were waited for; matrix products, arithmetic and copies ran while one was open for 0% of the time, Pallas kernels for 3%

profile of v5, /device:TPU:1, one launch (start us, length us, event | category | flops | bytes accessed | tf_op | source)
XLA Modules:
  0.0 119.8 jit_solution(17088926806515282914)
XLA Ops:
  0.6 29.5 %collective-permute-start = (f32[1,256]{1,0:T(1,128)}, f32[1,256]{1,0:T(1,128)S(1)}, u32[]{:S(2)}, u32[]{:S(2)}) collective-permute-start(f32[1,256]{1,0:T(1,128)} %bitcast.11), channel_id=1, source_target_pairs={{512,640},{520,648},{528,656},{536,664},{544,672},{552,680},{560,6... | collective-permute-start | bytes 3080 | tf_op jit(solution)/shard_map/ppermute | solution.py:183
  30.2 2.1 %collective-permute-done.token = f32[1,256]{1,0:T(1,128)S(1)} collective-permute-done((f32[1,256]{1,0:T(1,128)}, f32[1,256]{1,0:T(1,128)S(1)}, u32[]{:S(2)}, u32[]{:S(2)}) %collective-permute-start) | collective-permute-done | bytes 1056 | tf_op jit(solution)/shard_map/ppermute | solution.py:183
  32.2 0.0 copy-start.1
  32.2 2.6 %shard_map.93 = (bf16[512,512]{1,0:T(8,128)(2,1)S(1)}, bf16[256,128]{1,0:T(8,128)(2,1)S(1)}, f32[256,512]{1,0:T(8,128)S(1)}, bf16[256,2560]{1,0:T(8,128)(2,1)S(1)}, bf16[2560,512]{1,0:T(8,128)(2,1)S(1)}) custom-call(f32[1,256]{1,0:T(1,128)S(1)} %collective-permute-done.token, s32[2,128]{1,0:T(2,128)} %bitcast.16, bf16[128,512]{1,0:T(8,128)(2,1)} %cotangent_at.1, ...), custom_call_target="tpu_custom_call" | custom-call | tf_op jit(solution)/shard_map/pallas_call | solution.py:163
  34.9 62.3 %all_to_all.10 = bf16[64,8,512]{2,1,0:T(8,128)(2,1)S(1)} all-to-all(bf16[64,8,512]{2,1,0:T(8,128)(2,1)S(1)} %bitcast.10), channel_id=1, replica_groups=mesh['dp'=2,'expert'=64,'tensor'=8] {'expert'}, dimensions={0} | all-to-all | bytes 1048576 | tf_op jit(solution)/shard_map/all_to_all | solution.py:198
  97.2 0.0 copy-done.1
  97.2 1.8 %shard_map.95 = (bf16[256,512]{1,0:T(8,128)(2,1)S(1)}, bf16[8,336,256]{2,1,0:T(8,128)(2,1)}) custom-call(bf16[512,512]{1,0:T(8,128)(2,1)S(1)} %bitcast.8, bf16[2560,512]{1,0:T(8,128)(2,1)S(1)} %get-tuple-element.17.weight, f32[1,256]{1,0:T(1,128)S(1)} %bitcast.13, f32[256,512]{1,0:T(8,128)S(1)} %get-tuple-element.18.projected), custom_call_target="tpu_custom_call" | custom-call | tf_op jit(solution)/shard_map/pallas_call | solution.py:163
  99.0 6.4 %all-to-all-start.1 = ((bf16[8,336,256]{2,1,0:T(8,128)(2,1)}), bf16[8,336,256]{2,1,0:T(8,128)(2,1)S(1)}, u32[]{:S(2)}, u32[]{:S(2)}) async-start(bf16[8,336,256]{2,1,0:T(8,128)(2,1)} %get-tuple-element.19), calls=%async_computation.1 | async-start | bytes 2752512 | tf_op jit(solution)/shard_map/all_to_all | solution.py:209
  105.4 0.0 copy-start
  105.4 0.5 shard_map.96
  106.0 1.9 %collective-permute-start.1 = (bf16[640,512]{1,0:T(8,128)(2,1)S(1)}, bf16[640,512]{1,0:T(8,128)(2,1)S(1)}, u32[]{:S(2)}, u32[]{:S(2)}) collective-permute-start(bf16[640,512]{1,0:T(8,128)(2,1)S(1)} %get-tuple-element.22), channel_id=1, source_target_pairs={{0,512},{512,0},{1,513},{513,1},{2,514},{514,2},{3,515},{515,3},{4... | collective-permute-start | bytes 1966088 | tf_op jit(solution)/shard_map/ppermute | solution.py:211
  107.9 2.4 %collective-permute-start.2 = (bf16[640,512]{1,0:T(8,128)(2,1)S(1)}, bf16[640,512]{1,0:T(8,128)(2,1)S(1)}, u32[]{:S(2)}, u32[]{:S(2)}) collective-permute-start(bf16[640,512]{1,0:T(8,128)(2,1)S(1)} %get-tuple-element.23), channel_id=1, source_target_pairs={{0,512},{512,0},{1,513},{513,1},{2,514},{514,2},{3,515},{515,3},{4... | collective-permute-start | bytes 1966088 | tf_op jit(solution)/shard_map/ppermute | solution.py:211
  110.3 0.0 copy-done
  110.3 1.1 shard_map.94
  111.4 0.0 collective-permute-done.1.first
  111.4 0.6 collective-permute-done.2.second
  112.0 1.6 %shard_map.97.weight_grad_at = bf16[1280,512]{1,0:T(8,128)(2,1)} custom-call(bf16[256,2560]{1,0:T(8,128)(2,1)S(1)} %get-tuple-element.20.hidden, bf16[256,512]{1,0:T(8,128)(2,1)S(1)} %get-tuple-element.21.scaled, bf16[640,512]{1,0:T(8,128)(2,1)S(1)} %collective-permute-done.1.first, bf16[640,512]{1,0:T(8,128)(2,1)S(1)} %collective-permute-done.2.second), custom_call_target="tpu_custom_call" | custom-call | tf_op jit(solution)/shard_map/pallas_call | solution.py:163
  113.6 5.4 %all-to-all-done.1.partial = bf16[8,336,256]{2,1,0:T(8,128)(2,1)S(1)} async-done(((bf16[8,336,256]{2,1,0:T(8,128)(2,1)}), bf16[8,336,256]{2,1,0:T(8,128)(2,1)S(1)}, u32[]{:S(2)}, u32[]{:S(2)}) %all-to-all-start.1) | async-done | bytes 1376288 | tf_op jit(solution)/shard_map/all_to_all | solution.py:209
  119.0 0.8 shard_map.98
Async XLA Ops:
  0.6 31.6 %collective-permute-start = (f32[1,256]{1,0:T(1,128)}, f32[1,256]{1,0:T(1,128)S(1)}, u32[]{:S(2)}, u32[]{:S(2)}) collective-permute-start(f32[1,256]{1,0:T(1,128)} %bitcast.11), channel_id=1, source_target_pairs={{512,640},{520,648},{528,656},{536,664},{544,672},{552,680},{560,6... | collective-permute-start | bytes 3080 | tf_op jit(solution)/shard_map/ppermute | solution.py:183
  32.2 65.0 %copy-start.1 = (f32[256]{0:T(256)S(1)}, f32[256]{0:T(256)}, u32[]{:S(2)}) copy-start(f32[256]{0:T(256)} %param.9) | copy-start | bytes 3076
  99.0 20.0 %all-to-all-start.1 = ((bf16[8,336,256]{2,1,0:T(8,128)(2,1)}), bf16[8,336,256]{2,1,0:T(8,128)(2,1)S(1)}, u32[]{:S(2)}, u32[]{:S(2)}) async-start(bf16[8,336,256]{2,1,0:T(8,128)(2,1)} %get-tuple-element.19), calls=%async_computation.1 | async-start | bytes 2752512 | tf_op jit(solution)/shard_map/all_to_all | solution.py:209
  105.4 4.9 %copy-start = (bf16[128,512]{1,0:T(8,128)(2,1)S(1)}, bf16[128,512]{1,0:T(8,128)(2,1)}, u32[]{:S(2)}) copy-start(bf16[128,512]{1,0:T(8,128)(2,1)} %residual.1) | copy-start | bytes 393220
  106.0 5.5 %collective-permute-start.1 = (bf16[640,512]{1,0:T(8,128)(2,1)S(1)}, bf16[640,512]{1,0:T(8,128)(2,1)S(1)}, u32[]{:S(2)}, u32[]{:S(2)}) collective-permute-start(bf16[640,512]{1,0:T(8,128)(2,1)S(1)} %get-tuple-element.22), channel_id=1, source_target_pairs={{0,512},{512,0},{1,513},{513,1},{2,514},{514,2},{3,515},{515,3},{4... | collective-permute-start | bytes 1966088 | tf_op jit(solution)/shard_map/ppermute | solution.py:211
  107.9 4.1 %collective-permute-start.2 = (bf16[640,512]{1,0:T(8,128)(2,1)S(1)}, bf16[640,512]{1,0:T(8,128)(2,1)S(1)}, u32[]{:S(2)}, u32[]{:S(2)}) collective-permute-start(bf16[640,512]{1,0:T(8,128)(2,1)S(1)} %get-tuple-element.23), channel_id=1, source_target_pairs={{0,512},{512,0},{1,513},{513,1},{2,514},{514,2},{3,515},{515,3},{4... | collective-permute-start | bytes 1966088 | tf_op jit(solution)/shard_map/ppermute | solution.py:211
